TPU v7x, 512 devices: a whole 4x8x8 slice. The times are simulated.
512 devices in a mesh: cfg: 2 (over core), patch: 64 (over z_lo, x, y), head: 4 (over z_hi).
Axes of the slice: x: 4, y: 8, z: 8 (z_hi: 4, z_lo: 2; z = z_hi * 2 + z_lo), core: 2. Of those that a mesh axis runs over, the one named last changes fastest.
Arguments:
- queries: bfloat16 [2, 1536, 2560], P('cfg', 'patch', 'head'), may hold values from -180 to 180
- keys_new: bfloat16 [2, 1536, 2560], P('cfg', 'patch', 'head'), may hold values from -6 to 6
- values_new: bfloat16 [2, 1536, 2560], P('cfg', 'patch', 'head'), may hold values from -6 to 6
- cache_table: bfloat16 [2, 2, 256, 2560], P('cfg', None, None, 'head'), may hold values from -6 to 6
- exponents: int32 [2, 2, 192, 20], P('cfg', None, 'patch', 'head'), may hold values from -8 to -6
- patch_layout: int32 [1536], replicated, may hold values from 0 to 255
- out_weight: bfloat16 [2560, 2560], P('head'), may hold values from -0.125 to 0.125
- gate_table: float32 [50, 2560], P(None, ('cfg', 'head')), may hold values from 0.25 to 2
- timestep: int32 [1], replicated, may hold values from 0 to 49
Outputs:
- guided: bfloat16 [1536, 2560], P('patch', ('cfg', 'head'))
All inputs are finite; a program needn't handle non-finite values.
Results may differ from a plain program's by a relative error of at most 0.017.
The roundings to bfloat16 on the way count: a program that leaves them out, or rounds other values in their place, can miss the bound.
Values may be sent and summed in bfloat16 or wider, within the bound.
A program may use at most 64 MiB of HBM per device.

v0:
```python
import math

import jax
import jax.numpy as jnp
import numpy as np
from jax import lax
from jax.sharding import PartitionSpec as P

BLOCK = 8


def from_partner(value, axis, apart):
    mask = 2**apart
    pairs = [(source, source ^ mask) for source in range(lax.axis_size(axis))]
    return lax.ppermute(value, axis, pairs)


def power_two(exponent):
    powers_exp = np.arange(-12, 1)
    power_table = np.power(2.0, powers_exp).astype(np.float32)
    matches = exponent[..., None] == jnp.asarray(powers_exp, jnp.int32)
    return jnp.sum(
        jnp.where(matches, jnp.asarray(power_table, jnp.float32), jnp.float32(0.0)), axis=-1
    )


def expand_scale(exponent, head_dim):
    factor = power_two(exponent)
    factor = jnp.repeat(factor, BLOCK, axis=0)
    return jnp.repeat(factor, head_dim, axis=1)


def quantize(fresh_rows, cached, factor):
    difference = fresh_rows.astype(jnp.float32) - cached.astype(jnp.float32)
    scaled = jnp.clip(difference / factor, -448.0, 448.0).astype(jnp.bfloat16)
    return scaled * factor.astype(jnp.bfloat16)


def rebuild(cached, residual):
    return (cached.astype(jnp.float32) + residual.astype(jnp.float32)).astype(jnp.bfloat16)


def local(
    queries,
    keys_new,
    values_new,
    cache_table,
    exponents,
    patch_layout,
    out_weight,
    gate_table,
    timestep,
):
    own_queries = queries[0]
    tok_count, channel_count = own_queries.shape
    heads_here = exponents.shape[-1]
    head_dim = channel_count // heads_here
    key_table = cache_table[0, 0]
    value_table = cache_table[0, 1]
    own_first = lax.axis_index("patch") * tok_count
    own_rows = lax.dynamic_slice_in_dim(patch_layout, own_first, tok_count)
    key_residual = quantize(
        keys_new[0], jnp.take(key_table, own_rows, axis=0), expand_scale(exponents[0, 0], head_dim)
    )
    value_residual = quantize(
        values_new[0],
        jnp.take(value_table, own_rows, axis=0),
        expand_scale(exponents[0, 1], head_dim),
    )
    query_heads = own_queries.reshape(tok_count, heads_here, head_dim)
    inverse_root = 1.0 / math.sqrt(head_dim)

    def full_rows(table_half, shard_piece, first_row):
        row_count = shard_piece.shape[0]
        cache_rows = lax.dynamic_slice_in_dim(patch_layout, first_row, row_count)
        return rebuild(jnp.take(table_half, cache_rows, axis=0), shard_piece).reshape(
            row_count, heads_here, head_dim
        )

    key_full = full_rows(
        key_table, lax.all_gather(key_residual, "patch", axis=0, tiled=True), jnp.int32(0)
    )
    scores = (
        jnp.einsum("qhd,khd->hqk", query_heads, key_full, preferred_element_type=jnp.float32)
        * inverse_root
    )
    weights = jnp.exp(scores - jnp.max(scores, axis=-1, keepdims=True))
    totals = jnp.sum(weights, axis=-1)
    probs = weights.astype(jnp.bfloat16)
    shard_piece = lax.all_gather(value_residual, "patch", axis=0, tiled=True)
    first_row = jnp.int32(0)
    value_full = full_rows(value_table, shard_piece, first_row)
    prob_piece = lax.dynamic_slice_in_dim(probs, first_row, shard_piece.shape[0], 2)
    weighted = jnp.einsum(
        "hqk,khd->hqd", prob_piece, value_full, preferred_element_type=jnp.float32
    )
    attended = (
        (weighted / totals[..., None])
        .transpose(1, 0, 2)
        .reshape(tok_count, channel_count)
        .astype(jnp.bfloat16)
    )
    gate_row = jnp.take(gate_table, timestep, axis=0)[0]
    branch_index = lax.axis_index("cfg")
    is_conditional = branch_index == 0
    half_columns = out_weight.shape[1] // 2
    head_count = lax.axis_size("head")
    block_width = half_columns // head_count
    partial_value = jnp.dot(attended, out_weight, preferred_element_type=jnp.float32)
    arranged = (
        partial_value.reshape(tok_count, 2, head_count, block_width)
        .transpose(0, 2, 1, 3)
        .reshape(tok_count, 2 * half_columns)
    )
    summed = (
        lax.psum_scatter(arranged.astype(jnp.bfloat16), "head", scatter_dimension=1, tiled=True)
        .astype(jnp.float32)
        .reshape(tok_count, 2, block_width)
    )
    kept = lax.dynamic_index_in_dim(summed, branch_index, 1, keepdims=False)
    outgoing = lax.dynamic_index_in_dim(summed, 1 - branch_index, 1, keepdims=False)
    incoming = from_partner(outgoing, "cfg", 0)
    prediction = gate_row * kept
    partner = gate_row * incoming
    conditional = jnp.where(is_conditional, prediction, partner)
    unconditional = jnp.where(is_conditional, partner, prediction)
    guided = (unconditional + 5.0 * (conditional - unconditional)).astype(jnp.bfloat16)
    return guided


def solution(mesh):
    in_specs = (
        P("cfg", "patch", "head"),
        P("cfg", "patch", "head"),
        P("cfg", "patch", "head"),
        P("cfg", None, None, "head"),
        P("cfg", None, "patch", "head"),
        P(),
        P("head", None),
        P(None, ("cfg", "head")),
        P(),
    )
    out_specs = P("patch", ("cfg", "head"))
    return jax.shard_map(local, mesh=mesh, in_specs=in_specs, out_specs=out_specs, check_vma=False)
```

profile of v0, /device:TPU:1, one launch (start us, length us, event | category | flops | bytes accessed | tf_op | source)
XLA Modules:
  0.0 683.6 jit_solution(188643601110036895)
XLA Ops:
  6.5 0.0 copy-start.1
  6.5 0.0 copy-start.2
  6.5 0.0 copy-start.3
  6.5 0.0 all-gather.3.cloned.1.call-start
  6.5 0.8 compare_and_fusion.1
  7.4 1.1 slice_bitcast_fusion.1
  8.5 0.6 gather_fusion.1
  9.1 0.6 gather_fusion.3
  9.8 0.8 fusion.17
  10.5 0.1 copy.57
  10.6 0.1 copy.55
  10.7 0.8 select_reduce_fusion.1
  11.5 0.1 copy.65
  11.6 0.1 copy.66
  11.7 0.1 broadcast_in_dim.64
  11.8 0.1 broadcast_in_dim.67
  11.9 0.0 copy-done.2
  11.9 0.0 copy-done.3
  11.9 0.7 fusion.12
  12.7 0.0 all-gather.3.cloned.1.call-update
  12.7 0.0 all-gather.5.cloned.1.call-start
  12.7 0.7 all-gather.5.cloned.1.call-update
  13.4 0.0 reduce-scatter.4.cloned.1.call-start
  13.5 0.0 copy-done.1
  13.5 5.6 gather_fusion
  19.1 0.0 copy-start.4
  19.1 5.6 gather_fusion.2
  24.7 0.0 copy-done.4
  24.7 0.1 reshape_squeeze.3
  24.7 4.2 copy.50
  28.9 248.0 %all-gather.3.cloned.1.call-done = bf16[1536,640]{1,0:T(8,128)(2,1)} async-done(((bf16[24,640]{1,0:T(8,128)(2,1)}), bf16[1536,640]{1,0:T(8,128)(2,1)}) %all-gather.3.cloned.1.call-update) | async-done | bytes 1966096 | tf_op jit(solution)/shard_map/all_gather | solution.py:81
  276.9 301.8 %all-gather.5.cloned.1.call-done = bf16[1536,640]{1,0:T(8,128)(2,1)} async-done(((bf16[24,640]{1,0:T(8,128)(2,1)}), bf16[1536,640]{1,0:T(8,128)(2,1)}) %all-gather.5.cloned.1.call-update) | async-done | bytes 1966096 | tf_op jit(solution)/shard_map/all_gather | solution.py:90
  578.7 5.3 add_convert_fusion.1
  584.0 4.0 copy.42
  588.0 4.0 copy.47
  592.1 0.0 copy-start
  592.1 2.1 fusion.18
  594.2 0.2 fusion.4
  594.5 0.0 copy-done
  594.5 0.7 fusion.3
  595.2 0.1 reshape.143
  595.3 1.2 fusion.1
  596.5 1.1 copy.61
  597.6 0.0 reduce-scatter.4.cloned.1.call-update
  597.6 72.7 %reduce-scatter.4.cloned.1.call-done = bf16[640,24]{1,0:T(8,128)(2,1)} async-done(((bf16[2560,24]{1,0:T(8,128)(2,1)}), bf16[640,24]{1,0:T(8,128)(2,1)}) %reduce-scatter.4.cloned.1.call-update) | async-done | bytes 30736
  670.3 1.0 copy.60
  671.3 0.1 reshape.91
  671.5 0.1 constant_dynamic-slice_fusion.1
  671.6 3.4 collective-permute-start
  675.7 0.7 fusion.16
  676.4 0.0 collective-permute-done
  676.4 0.6 add_convert_fusion.2
  (8 shorter events, 0.1 us)
Async XLA Ops:
  6.5 7.0 %copy-start.1 = (s32[1536]{0:T(1024)S(1)}, s32[1536]{0:T(1024)}, u32[]{:S(2)}) copy-start(s32[1536]{0:T(1024)} %param.22) | copy-start | bytes 18436
  6.5 5.4 copy-start.2
  6.5 5.4 copy-start.3
  6.5 270.4 %all-gather.3.cloned.1.call-start = ((), (), s32[]{:S(2)}) async-start(), calls=%async_computation.1 | async-start | bytes 1996800 | tf_op jit(solution)/shard_map/all_gather | solution.py:81
  12.7 566.0 %all-gather.5.cloned.1.call-start = ((), (), s32[]{:S(2)}) async-start(), calls=%async_computation.2 | async-start | bytes 1996800 | tf_op jit(solution)/shard_map/all_gather | solution.py:90
  13.4 656.9 %reduce-scatter.4.cloned.1.call-start = ((), (), s32[]{:S(2)}) async-start(), calls=%async_computation.3 | async-start | bytes 819200
  19.1 5.6 copy-start.4
  592.1 2.4 copy-start
  671.6 4.8 collective-permute-start
Sparse Core Ops, SparseCore 0:
  12.8 264.0 all-gather.2
  279.0 299.6 all-gather.4
  597.8 72.5 reduce-scatter.3
where the time goes:
time: 684 us
  waiting for transfers between devices  623 us (91%)
  local copies, waits for them, and re-layouts  29.6 us (4%)
  between operations  13.9 us (2%)
  other arithmetic  9.34 us (1%)
    all_gather x1, waiting for transfers between devices, local(): shard_piece = lax.all_gather(value_residual, 'patch', axis=0, tiled=True)  302 us
    all_gather x1, waiting for transfers between devices, local(): lax.all_gather(key_residual, 'patch', axis=0, tiled=True)  248 us
    unnamed x4, waiting for transfers between devices  73.4 us
  transfers between devices with their start and end apart: 4, of which 3 were waited for; matrix products, arithmetic and copies ran while one was open for 2% of the time, Pallas kernels for 0%

commit v1 on v0

v1 whole, which is shorter than its diff:
```python
import functools
import math

import jax
import jax.numpy as jnp
from jax import lax
from jax.experimental import pallas as pl
from jax.experimental.pallas import tpu as pltpu
from jax.sharding import PartitionSpec as P

MESH = pl.DeviceIdType.MESH
BLOCK = 8
LANES = 128
GRID = (2, 4, 8)

F32 = jnp.float32
BF16 = jnp.bfloat16


def dot_t(a, b):
    return lax.dot_general(a, b, (((1,), (1,)), ((), ())), preferred_element_type=F32)


def kernel(
    n_head,
    layout,
    exponents,
    timestep,
    queries,
    keys_new,
    values_new,
    cache_table,
    out_weight,
    gate_table,
    out,
    q_in,
    k_in,
    v_in,
    table,
    weight,
    gate,
    q_all,
    kv_all,
    o_send,
    o_recv,
    a_buf,
    g_send,
    g_recv,
    local_sem,
    q_ssem,
    q_rsem,
    kv_ssem,
    kv_rsem,
    o_ssem,
    o_rsem,
    a_sem,
    g_ssem,
    g_rsem,
):
    nz, nx, ny = GRID
    nxz = nz * nx
    tok, channels = q_in.shape
    heads = channels // LANES
    rows = tok * heads
    blocks = tok // BLOCK
    half = weight.shape[1]
    width = out.shape[1]

    cfg = lax.axis_index("cfg")
    patch = lax.axis_index("patch")
    head = lax.axis_index("head")
    y = lax.rem(patch, ny)
    xz = lax.div(patch, ny)
    x = lax.rem(xz, nx)
    z = lax.div(xz, nx)

    def y_partner(step):
        return (cfg, xz * ny + lax.rem(y + step + ny, ny), head)

    def xz_partner(dz, dx):
        other_z = lax.rem(z + dz, nz)
        other_x = lax.rem(x + dx + nx, nx)
        return (cfg, (other_z * nx + other_x) * ny + y, head)

    def head_partner(step):
        return (cfg, patch, lax.rem(head + step + n_head, n_head))

    other_core = (1 - cfg, patch, head)

    local = [
        pltpu.make_async_copy(cache_table, table, local_sem.at[0]),
        pltpu.make_async_copy(keys_new, k_in, local_sem.at[1]),
        pltpu.make_async_copy(values_new, v_in, local_sem.at[2]),
        pltpu.make_async_copy(queries, q_in, local_sem.at[3]),
        pltpu.make_async_copy(
            out_weight.at[:, pl.ds(pl.multiple_of(cfg * half, LANES), half)], weight, local_sem.at[4]
        ),
        pltpu.make_async_copy(gate_table, gate, local_sem.at[5]),
    ]
    for copy in local:
        copy.start()

    partners = [y_partner(s) for s in range(1, ny)]
    partners += [xz_partner(dz, dx) for dz in range(nz) for dx in range(nx) if dz or dx]
    partners += [head_partner(s) for s in range(1, n_head)]
    partners += [other_core]
    barrier = pltpu.get_barrier_semaphore()
    for partner in partners:
        pl.semaphore_signal(barrier, inc=1, device_id=partner, device_id_type=MESH)

    local[3].wait()
    own_q = q_in[...].astype(F32)
    pad = jnp.zeros((BLOCK, LANES), F32)
    q_rows = [own_q[:, h * LANES : (h + 1) * LANES] for h in range(heads)]
    q_all[0] = jnp.concatenate(q_rows + [pad], axis=0).astype(BF16)

    lane = lax.broadcasted_iota(jnp.int32, (BLOCK, table.shape[1]), 1)
    sub = lax.broadcasted_iota(jnp.int32, (BLOCK, table.shape[1]), 0)
    picks = []
    for b in range(blocks):
        wanted = jnp.zeros(lane.shape, jnp.int32)
        for i in range(BLOCK):
            wanted = jnp.where(sub == i, layout[patch * tok + b * BLOCK + i], wanted)
        picks.append(jnp.where(lane == wanted, 1.0, 0.0).astype(F32))
    onehot = jnp.concatenate(picks, axis=0).astype(BF16)

    local[0].wait()
    local[1].wait()
    local[2].wait()
    full = []
    for kind, fresh_ref in enumerate((k_in, v_in)):
        cached = jnp.dot(onehot, table[kind], preferred_element_type=F32)
        fresh = fresh_ref[...].astype(F32)
        for h in range(heads):
            for b in range(blocks):
                power = exponents[(kind * blocks + b) * heads + h]
                factor = jnp.where(power == -8, 2.0**-8, jnp.where(power == -7, 2.0**-7, 2.0**-6))
                inverse = jnp.where(power == -8, 2.0**8, jnp.where(power == -7, 2.0**7, 2.0**6))
                where = (slice(b * BLOCK, (b + 1) * BLOCK), slice(h * LANES, (h + 1) * LANES))
                old = cached[where]
                scaled = jnp.clip((fresh[where] - old) * inverse, -448.0, 448.0)
                residual = scaled.astype(BF16).astype(F32) * factor
                full.append(old + residual)
    kv_all[0] = jnp.concatenate(full, axis=0).astype(BF16)

    pl.semaphore_wait(barrier, len(partners))

    sends = []
    for dz in reversed(range(nz)):
        for dx in range(nx):
            if dz or dx:
                e = dz * nx + dx
                copy = pltpu.make_async_remote_copy(
                    src_ref=kv_all.at[0],
                    dst_ref=kv_all.at[e],
                    send_sem=kv_ssem.at[e],
                    recv_sem=kv_rsem.at[e],
                    device_id=xz_partner(dz, dx),
                    device_id_type=MESH,
                )
                copy.start()
                sends.append(copy)
    for s in range(1, ny):
        copy = pltpu.make_async_remote_copy(
            src_ref=q_all.at[0],
            dst_ref=q_all.at[s],
            send_sem=q_ssem.at[s],
            recv_sem=q_rsem.at[s],
            device_id=y_partner(s),
            device_id_type=MESH,
        )
        copy.start()
        sends.append(copy)
    for copy in sends:
        copy.wait_recv()

    inverse_root = 1.0 / math.sqrt(LANES)
    q_f = [q_all[s].astype(F32) for s in range(ny)]
    kv_f = [kv_all[e].astype(F32) for e in range(nxz)]
    outs, lses = [], []
    for h in range(heads):
        k0, v0 = h * tok, rows + h * tok
        q_h = jnp.concatenate([q[k0 : k0 + tok] for q in q_f], axis=0).astype(BF16)
        k_h = jnp.concatenate([kv[k0 : k0 + tok] for kv in kv_f], axis=0).astype(BF16)
        v_h = jnp.concatenate([kv[v0 : v0 + tok] for kv in kv_f], axis=0).astype(BF16)
        scores = dot_t(q_h, k_h) * inverse_root
        top = jnp.max(scores, axis=1, keepdims=True)
        weights = jnp.exp(scores - top)
        total = jnp.sum(weights, axis=1, keepdims=True)
        mixed = jnp.dot(weights.astype(BF16), v_h, preferred_element_type=F32)
        outs.append(mixed / total)
        lses.append(top + jnp.log(total))

    eye = lax.broadcasted_iota(jnp.int32, (rows, LANES), 0) == lax.broadcasted_iota(
        jnp.int32, (rows, LANES), 1
    )
    sub8 = lax.broadcasted_iota(jnp.int32, (BLOCK, LANES), 0)
    o_sends = []
    for s in list(range(1, ny)) + [0]:
        part = slice(s * tok, (s + 1) * tok)
        lse = jnp.concatenate([v[part] for v in lses], axis=0)
        lse = jnp.sum(jnp.where(eye, lse, 0.0), axis=0, keepdims=True)
        high = lse.astype(BF16).astype(F32)
        mid = (lse - high).astype(BF16).astype(F32)
        low = lse - high - mid
        stats = jnp.where(sub8 == 0, high, jnp.where(sub8 == 1, mid, jnp.where(sub8 == 2, low, 0.0)))
        message = jnp.concatenate([o[part] for o in outs] + [stats], axis=0).astype(BF16)
        if s == 0:
            o_recv[0] = message
        else:
            o_send[s] = message
            copy = pltpu.make_async_remote_copy(
                src_ref=o_send.at[s],
                dst_ref=o_recv.at[s],
                send_sem=o_ssem.at[s],
                recv_sem=o_rsem.at[s],
                device_id=y_partner(-s),
                device_id_type=MESH,
            )
            copy.start()
            o_sends.append(copy)
    for copy in o_sends:
        copy.wait_recv()

    o_f = [o_recv[s].astype(F32) for s in range(ny)]
    lse_rows = []
    for o in o_f:
        stats = o[rows : rows + BLOCK]
        lse_rows.append(stats[0:1] + stats[1:2] + stats[2:3])
    top = functools.reduce(jnp.maximum, lse_rows)
    shares = [jnp.exp(v - top) for v in lse_rows]
    total = functools.reduce(jnp.add, shares)
    attended = jnp.zeros((rows, LANES), F32)
    for o, share in zip(o_f, shares):
        column = jnp.sum(jnp.where(eye, share / total, 0.0), axis=1, keepdims=True)
        attended = attended + o[:rows] * column
    a_buf[0] = jnp.concatenate([attended, pad], axis=0).astype(BF16)

    a_copy = pltpu.make_async_remote_copy(
        src_ref=a_buf.at[0],
        dst_ref=a_buf.at[1],
        send_sem=a_sem.at[0],
        recv_sem=a_sem.at[1],
        device_id=other_core,
        device_id_type=MESH,
    )
    a_copy.start()
    local[4].wait()
    local[5].wait()
    a_copy.wait_recv()

    own_a = a_buf[0].astype(F32)
    other_a = a_buf[1].astype(F32)
    stacked = jnp.concatenate(
        [
            jnp.concatenate([own_a[h * tok : (h + 1) * tok], other_a[h * tok : (h + 1) * tok]], axis=0)
            for h in range(heads)
        ],
        axis=1,
    ).astype(BF16)
    projected = jnp.dot(stacked, weight[...], preferred_element_type=F32)
    own_p, other_p = projected[:tok], projected[tok:]
    first = cfg == 0
    conditional = jnp.where(first, own_p, other_p)
    unconditional = jnp.where(first, other_p, own_p)
    mixed = unconditional + 5.0 * (conditional - unconditional)
    chunks = pl.cdiv(width, LANES)
    mixed = jnp.concatenate([mixed, jnp.zeros((tok, LANES), F32)], axis=1)
    for k in range(n_head):
        first_col = k * width
        pieces = [
            mixed[:, first_col + c * LANES : first_col + (c + 1) * LANES] for c in range(chunks)
        ]
        g_send[k] = jnp.concatenate(pieces + [pad], axis=0).astype(BF16)
    g_sends = []
    for s in range(1, n_head):
        copy = pltpu.make_async_remote_copy(
            src_ref=g_send.at[lax.rem(head + s, n_head)],
            dst_ref=g_recv.at[s],
            send_sem=g_ssem.at[s],
            recv_sem=g_rsem.at[s],
            device_id=head_partner(s),
            device_id_type=MESH,
        )
        copy.start()
        g_sends.append(copy)
    summed = g_send[head].astype(F32)
    for s, copy in enumerate(g_sends):
        copy.wait_recv()
        summed = summed + g_recv[s + 1].astype(F32)
    here = lax.broadcasted_iota(jnp.int32, gate.shape, 0) == timestep[0]
    gate_row = jnp.sum(jnp.where(here, gate[...], 0.0), axis=0, keepdims=True)
    for c in range(chunks):
        lanes = min(LANES, width - c * LANES)
        cols = slice(c * LANES, c * LANES + lanes)
        part = summed[c * tok : (c + 1) * tok, :lanes] * gate_row[:, cols]
        out[:, cols] = part.astype(out.dtype)

    for copy in sends + o_sends + [a_copy] + g_sends:
        copy.wait_send()


def solution(mesh):
    n_head = mesh.shape["head"]

    def local(
        queries,
        keys_new,
        values_new,
        cache_table,
        exponents,
        patch_layout,
        out_weight,
        gate_table,
        timestep,
    ):
        nz, nx, ny = GRID
        nxz = nz * nx
        _, tok, channels = queries.shape
        heads = channels // LANES
        rows = tok * heads
        dout = out_weight.shape[1]
        width = dout // 2 // n_head
        q_rows = rows + BLOCK
        g_rows = pl.cdiv(width, LANES) * tok + BLOCK
        any_spec = pl.BlockSpec(memory_space=pl.ANY)
        smem_spec = pl.BlockSpec(memory_space=pltpu.SMEM)
        dma = pltpu.SemaphoreType.DMA
        return pl.pallas_call(
            functools.partial(kernel, n_head),
            out_shape=jax.ShapeDtypeStruct((tok, width), BF16),
            in_specs=[smem_spec] * 3 + [any_spec] * 6,
            out_specs=pl.BlockSpec(memory_space=pltpu.VMEM),
            scratch_shapes=[
                pltpu.VMEM((tok, channels), BF16),
                pltpu.VMEM((tok, channels), BF16),
                pltpu.VMEM((tok, channels), BF16),
                pltpu.VMEM(cache_table.shape[1:], BF16),
                pltpu.VMEM((channels, dout // 2), BF16),
                pltpu.VMEM(gate_table.shape, F32),
                pltpu.VMEM((ny, q_rows, LANES), BF16),
                pltpu.VMEM((nxz, 2 * rows, LANES), BF16),
                pltpu.VMEM((ny, q_rows, LANES), BF16),
                pltpu.VMEM((ny, q_rows, LANES), BF16),
                pltpu.VMEM((2, q_rows, LANES), BF16),
                pltpu.VMEM((n_head, g_rows, LANES), BF16),
                pltpu.VMEM((n_head, g_rows, LANES), BF16),
                dma((6,)),
                dma((ny,)),
                dma((ny,)),
                dma((nxz,)),
                dma((nxz,)),
                dma((ny,)),
                dma((ny,)),
                dma((2,)),
                dma((n_head,)),
                dma((n_head,)),
            ],
            compiler_params=pltpu.CompilerParams(
                collective_id=0, has_side_effects=True, vmem_limit_bytes=60 * 2**20
            ),
        )(
            patch_layout,
            exponents.reshape(-1),
            timestep,
            queries[0],
            keys_new[0],
            values_new[0],
            cache_table[0],
            out_weight,
            gate_table,
        )

    in_specs = (
        P("cfg", "patch", "head"),
        P("cfg", "patch", "head"),
        P("cfg", "patch", "head"),
        P("cfg", None, None, "head"),
        P("cfg", None, "patch", "head"),
        P(),
        P("head", None),
        P(None, ("cfg", "head")),
        P(),
    )
    out_specs = P("patch", ("cfg", "head"))
    return jax.shard_map(local, mesh=mesh, in_specs=in_specs, out_specs=out_specs, check_vma=False)
```

time: 684 us -> 42.9 us (0.06)
  waiting for transfers between devices: 623 us -> 0 us
  Pallas kernels: 0 us -> 39.3 us
  local copies, waits for them, and re-layouts: 29.6 us -> 2.61 us
  between operations: 13.9 us -> 0.66 us
  other arithmetic: 9.34 us -> 0 us
    all_gather x2 -> x0, waiting for transfers between devices: 550 us -> none  [the longest x1 302 us: local(): shard_piece = lax.all_gather(value_residual, 'patch', axis=0, tiled=True)]
    unnamed x4 -> x0, waiting for transfers between devices: 73.4 us -> none
    pallas_call x0 -> x1, Pallas kernels: none -> 39.3 us  [local(): pl.pallas_call(functools.partial(kernel, n_head), out_shape=jax.ShapeDtyp...]
    gather x4 -> x0, local copies, waits for them, and re-layouts: 12.4 us -> none  [the longest x2 11.1 us: full_rows(): jnp.take(table_half, cache_rows, axis=0)]
    convert_element_type x4 -> x0, local copies, waits for them, and re-layouts: 8.16 us -> none  [the longest x2 8.08 us: rebuild(): (cached.astype(jnp.float32) + residual.astype(jnp.float32)).astype(jnp.bf...]
  transfers between devices with their start and end apart: 4 -> 0, of which waited for: 3 -> 0; matrix products, arithmetic and copies ran while one was open for 2% -> 0% of each run, Pallas kernels for 0% -> 0%
where the time goes in v1:
time: 42.9 us; the launch traced here: 42.6 us
  Pallas kernels  39.3 us (92%)
  local copies, waits for them, and re-layouts  2.61 us (6%)
  between operations  0.66 us (2%)
    pallas_call x1, Pallas kernels, local(): pl.pallas_call(functools.partial(kernel, n_head), out_shape=jax.ShapeDtyp...  39.3 us
    unnamed x2, local copies, waits for them, and re-layouts  2.02 us

profile of v1, /device:TPU:1, one launch (start us, length us, event | category | flops | bytes accessed | tf_op | source)
XLA Modules:
  0.0 42.6 jit_solution(7390726321055339136)
XLA Ops:
  0.7 0.7 %copy.11 = s32[1,2,3,5]{3,2,1,0:T(4,128)S(1)} copy(s32[1,2,3,5]{3,1,2,0:T(2,128)} %param.13) | data formatting | bytes 240 | tf_op args[4]
  1.3 0.6 %reshape.3.exponents = s32[30]{0:T(128)} reshape(s32[1,2,3,5]{3,2,1,0:T(4,128)S(1)} %copy.11) | data formatting | bytes 240 | tf_op jit(solution)/shard_map/reshape | solution.py:364
  1.9 39.3 %shard_map.91 = bf16[24,320]{1,0:T(8,128)(2,1)} custom-call(s32[1536]{0:T(1024)} %layout.1, s32[30]{0:T(128)} %reshape.3.exponents, s32[1]{0:T(128)S(6)} %copy.13.timestep, bf16[24,640]{1,0:T(8,128)(2,1)} %bitcast.5, bf16[24,640]{1,0:T(8,128)(2,1)} %bitcast.6, bf16[24,640]{1,0:T(8,128)(2,1)} %bitcast.7, bf16[2,256,640]{2,1,0:T(8,128)(2,1)} %bitcast.4, ...), custom_call_target="tpu_custom_call" | custom-call | tf_op jit(solution)/shard_map/pallas_call | solution.py:329
  41.3 1.3 %copy.14 = bf16[24,320]{1,0:T(8,128)(2,1)} copy(bf16[24,320]{1,0:T(8,128)(2,1)} %shard_map.91) | data formatting | bytes 30720

commit v2 on v1

v2 whole, which is shorter than its diff:
```python
import functools
import math

import jax
import jax.numpy as jnp
from jax import lax
from jax.experimental import pallas as pl
from jax.experimental.pallas import tpu as pltpu
from jax.sharding import PartitionSpec as P

MESH = pl.DeviceIdType.MESH
BLOCK = 8
LANES = 128
GRID = (2, 4, 8)

F32 = jnp.float32
BF16 = jnp.bfloat16


def dot_t(a, b):
    return lax.dot_general(a, b, (((1,), (1,)), ((), ())), preferred_element_type=F32)


def far_first(count):
    return sorted(range(1, count), key=lambda step: -min(step, count - step))


def padded(count):
    return -(-count // 16) * 16


def kernel(
    n_head,
    chunks,
    layout_in,
    exponents_in,
    timestep_in,
    queries,
    keys_new,
    values_new,
    cache_table,
    out_weight,
    gate_table,
    out,
    layout,
    exponents,
    timestep,
    q_in,
    k_in,
    v_in,
    table,
    weight,
    gate,
    q_all,
    kv_all,
    o_send,
    o_recv,
    a_buf,
    projected,
    g_send,
    g_recv,
    local_sem,
    q_ssem,
    q_rsem,
    kv_ssem,
    kv_rsem,
    o_ssem,
    o_rsem,
    a_ssem,
    a_rsem,
    g_ssem,
    g_rsem,
):
    nz, nx, ny = GRID
    nxz = nz * nx
    tok = q_in.shape[0]
    heads = q_in.shape[1] // LANES
    blocks = tok // BLOCK
    half = weight.shape[1]
    width = out.shape[1]

    cfg = lax.axis_index("cfg")
    patch = lax.axis_index("patch")
    head = lax.axis_index("head")
    y = lax.rem(patch, ny)
    xz = lax.div(patch, ny)
    x = lax.rem(xz, nx)
    z = lax.div(xz, nx)

    def y_partner(step):
        return (cfg, xz * ny + lax.rem(y + step + ny, ny), head)

    def xz_partner(dz, dx):
        other_z = lax.rem(z + dz, nz)
        other_x = lax.rem(x + dx, nx)
        return (cfg, (other_z * nx + other_x) * ny + y, head)

    def head_partner(step):
        return (cfg, patch, lax.rem(head + step, n_head))

    def send(src, dst, ssem, rsem, device):
        copy = pltpu.make_async_remote_copy(
            src_ref=src,
            dst_ref=dst,
            send_sem=ssem,
            recv_sem=rsem,
            device_id=device,
            device_id_type=MESH,
        )
        copy.start()
        return copy

    other_core = (1 - cfg, patch, head)
    y_steps = far_first(ny)
    xz_steps = [(1, dx) for dx in far_first(nx)] if nz > 1 else []
    xz_steps += [(0, dx) for dx in far_first(nx)]
    xz_steps += [(1, 0)] if nz > 1 else []
    head_steps = far_first(n_head)

    partners = [y_partner(s) for s in y_steps] + [xz_partner(*s) for s in xz_steps]
    partners += [head_partner(s) for s in head_steps] + [other_core]
    barrier = pltpu.get_barrier_semaphore()
    for partner in partners:
        pl.semaphore_signal(barrier, inc=1, device_id=partner, device_id_type=MESH)
    pairs = [
        (queries, q_in),
        (layout_in, layout),
        (exponents_in, exponents),
        (cache_table, table),
        (keys_new, k_in),
        (values_new, v_in),
        (timestep_in, timestep),
        (gate_table, gate),
        (out_weight.at[:, pl.ds(pl.multiple_of(cfg * half, LANES), half)], weight),
    ]
    local = [pltpu.make_async_copy(a, b, local_sem.at[i]) for i, (a, b) in enumerate(pairs)]
    for copy in local[:6]:
        copy.start()

    local[0].wait()
    own_q = q_in[...].astype(F32)
    for c, (first, last) in enumerate(chunks):
        rows = [own_q[:, h * LANES : (h + 1) * LANES] for h in range(first, last)]
        extra = q_all[c].shape[1] - (last - first) * tok
        rows += [jnp.zeros((extra, LANES), F32)] if extra else []
        q_all[c][0] = jnp.concatenate(rows, axis=0).astype(BF16)

    local[1].wait()
    lane = lax.broadcasted_iota(jnp.int32, (BLOCK, table.shape[1]), 1)
    sub = lax.broadcasted_iota(jnp.int32, (BLOCK, table.shape[1]), 0)
    picks = []
    for b in range(blocks):
        wanted = jnp.zeros(lane.shape, jnp.int32)
        for i in range(BLOCK):
            wanted = jnp.where(sub == i, layout[patch * tok + b * BLOCK + i], wanted)
        picks.append(jnp.where(lane == wanted, 1.0, 0.0).astype(F32))
    onehot = jnp.concatenate(picks, axis=0).astype(BF16)

    for copy in local[2:6]:
        copy.wait()
    full = [[], []]
    for kind, fresh_ref in enumerate((k_in, v_in)):
        cached = jnp.dot(onehot, table[kind], preferred_element_type=F32)
        fresh = fresh_ref[...].astype(F32)
        for h in range(heads):
            for b in range(blocks):
                power = exponents[b, kind, h]
                factor = jnp.where(power == -8, 2.0**-8, jnp.where(power == -7, 2.0**-7, 2.0**-6))
                inverse = jnp.where(power == -8, 2.0**8, jnp.where(power == -7, 2.0**7, 2.0**6))
                where = (slice(b * BLOCK, (b + 1) * BLOCK), slice(h * LANES, (h + 1) * LANES))
                old = cached[where]
                scaled = jnp.clip((fresh[where] - old) * inverse, -448.0, 448.0)
                residual = scaled.astype(BF16).astype(F32) * factor
                full[kind].append(old + residual)
    for c, (first, last) in enumerate(chunks):
        part = slice(first * blocks, last * blocks)
        kv_all[c][0] = jnp.concatenate(full[0][part] + full[1][part], axis=0).astype(BF16)

    pl.semaphore_wait(barrier, len(partners))

    gathers = []
    for c in range(len(chunks)):
        copies = []
        for y_step, xz_step in zip(y_steps, xz_steps):
            q, kv = q_all[c], kv_all[c]
            slot = xz_step[0] * nx + xz_step[1]
            copies += [
                send(q.at[0], q.at[y_step], q_ssem.at[c, y_step], q_rsem.at[c, y_step], y_partner(y_step)),
                send(kv.at[0], kv.at[slot], kv_ssem.at[c, slot], kv_rsem.at[c, slot], xz_partner(*xz_step)),
            ]
        gathers.append(copies)
    for copy in local[6:]:
        copy.start()

    inverse_root = 1.0 / math.sqrt(LANES)
    sub8 = lax.broadcasted_iota(jnp.int32, (BLOCK, LANES), 0)

    def diagonal(rows):
        shape = (rows, LANES)
        return lax.broadcasted_iota(jnp.int32, shape, 0) == lax.broadcasted_iota(jnp.int32, shape, 1)

    o_sends = []
    for c, (first, last) in enumerate(chunks):
        for copy in gathers[c]:
            copy.wait_recv()
        rows = (last - first) * tok
        eye = diagonal(rows)
        q_f = [q_all[c][s].astype(F32) for s in range(ny)]
        kv_f = [kv_all[c][e].astype(F32) for e in range(nxz)]
        outs, lses = [], []
        for h in range(last - first):
            k0, v0 = h * tok, rows + h * tok
            q_h = jnp.concatenate([q[k0 : k0 + tok] for q in q_f], axis=0).astype(BF16)
            k_h = jnp.concatenate([kv[k0 : k0 + tok] for kv in kv_f], axis=0).astype(BF16)
            v_h = jnp.concatenate([kv[v0 : v0 + tok] for kv in kv_f], axis=0).astype(BF16)
            scores = dot_t(q_h, k_h) * inverse_root
            top = jnp.max(scores, axis=1, keepdims=True)
            weights = jnp.exp(scores - top)
            total = jnp.sum(weights, axis=1, keepdims=True)
            mixed = jnp.dot(weights.astype(BF16), v_h, preferred_element_type=F32)
            outs.append(mixed / total)
            lses.append(top + jnp.log(total))
        copies = []
        for s in y_steps + [0]:
            part = slice(s * tok, (s + 1) * tok)
            lse = jnp.concatenate([v[part] for v in lses], axis=0)
            lse = jnp.sum(jnp.where(eye, lse, 0.0), axis=0, keepdims=True)
            high = lse.astype(BF16).astype(F32)
            mid = (lse - high).astype(BF16).astype(F32)
            low = lse - high - mid
            stats = jnp.where(sub8 == 0, high, jnp.where(sub8 == 1, mid, jnp.where(sub8 == 2, low, 0.0)))
            extra = o_recv[c].shape[1] - rows - BLOCK
            pad = [jnp.zeros((extra, LANES), F32)] if extra else []
            message = jnp.concatenate([o[part] for o in outs] + [stats] + pad, axis=0).astype(BF16)
            if s == 0:
                o_recv[c][0] = message
            else:
                o_send[c][s] = message
                copies.append(
                    send(o_send[c].at[s], o_recv[c].at[s], o_ssem.at[c, s], o_rsem.at[c, s], y_partner(-s))
                )
        o_sends.append(copies)

    for copy in local[6:]:
        copy.wait()
    a_sends = []
    for c, (first, last) in enumerate(chunks):
        for copy in o_sends[c]:
            copy.wait_recv()
        rows = (last - first) * tok
        eye = diagonal(rows)
        o_f = [o_recv[c][s].astype(F32) for s in range(ny)]
        lse_rows = []
        for o in o_f:
            lse_rows.append(o[rows : rows + 1] + o[rows + 1 : rows + 2] + o[rows + 2 : rows + 3])
        top = functools.reduce(jnp.maximum, lse_rows)
        shares = [jnp.exp(v - top) for v in lse_rows]
        total = functools.reduce(jnp.add, shares)
        attended = jnp.zeros((rows, LANES), F32)
        for o, share in zip(o_f, shares):
            column = jnp.sum(jnp.where(eye, share / total, 0.0), axis=1, keepdims=True)
            attended = attended + o[:rows] * column
        extra = a_buf[c].shape[1] - rows
        pad = [jnp.zeros((extra, LANES), F32)] if extra else []
        a_buf[c][0] = jnp.concatenate([attended] + pad, axis=0).astype(BF16)
        swap = send(a_buf[c].at[0], a_buf[c].at[1], a_ssem.at[c], a_rsem.at[c], other_core)
        a_sends.append(swap)
        swap.wait_recv()
        own_a = a_buf[c][0].astype(F32)
        other_a = a_buf[c][1].astype(F32)
        stacked = []
        for h in range(last - first):
            part = slice(h * tok, (h + 1) * tok)
            stacked.append(jnp.concatenate([own_a[part], other_a[part]], axis=0))
        product = jnp.dot(
            jnp.concatenate(stacked, axis=1).astype(BF16),
            weight[first * LANES : last * LANES, :],
            preferred_element_type=F32,
        )
        if c < len(chunks) - 1:
            projected[...] = product if c == 0 else projected[...] + product
    product = product + projected[...]
    own_p, other_p = product[:tok], product[tok:]
    conditional = jnp.where(cfg == 0, own_p, other_p)
    unconditional = jnp.where(cfg == 0, other_p, own_p)
    mixed = unconditional + 5.0 * (conditional - unconditional)

    n_cols = pl.cdiv(width, LANES)
    mixed = jnp.concatenate([mixed, jnp.zeros((tok, LANES), F32)], axis=1)
    extra = g_send.shape[1] - n_cols * tok
    pad = [jnp.zeros((extra, LANES), F32)] if extra else []
    for k in range(n_head):
        starts = [k * width + i * LANES for i in range(n_cols)]
        g_send[k] = jnp.concatenate([mixed[:, i : i + LANES] for i in starts] + pad, axis=0).astype(BF16)
    g_sends = [
        send(g_send.at[lax.rem(head + s, n_head)], g_recv.at[s], g_ssem.at[s], g_rsem.at[s], head_partner(s))
        for s in head_steps
    ]
    here = lax.broadcasted_iota(jnp.int32, gate.shape, 0) == timestep[0]
    gate_row = jnp.sum(jnp.where(here, gate[...], 0.0), axis=0, keepdims=True)
    summed = g_send[head].astype(F32)
    for s, copy in zip(head_steps, g_sends):
        copy.wait_recv()
        summed = summed + g_recv[s].astype(F32)
    for i in range(n_cols):
        lanes = min(LANES, width - i * LANES)
        cols = slice(i * LANES, i * LANES + lanes)
        part = summed[i * tok : (i + 1) * tok, :lanes] * gate_row[:, cols]
        out[:, cols] = part.astype(out.dtype)

    for copy in sum(gathers + o_sends, []) + a_sends + g_sends:
        copy.wait_send()


def solution(mesh):
    n_head = mesh.shape["head"]

    def local(
        queries,
        keys_new,
        values_new,
        cache_table,
        exponents,
        patch_layout,
        out_weight,
        gate_table,
        timestep,
    ):
        nz, nx, ny = GRID
        nxz = nz * nx
        _, tok, channels = queries.shape
        heads = channels // LANES
        dout = out_weight.shape[1]
        width = dout // 2 // n_head
        chunks = [(0, (heads + 1) // 2), ((heads + 1) // 2, heads)]
        counts = [(last - first) * tok for first, last in chunks]
        q_rows = [padded(n) for n in counts]
        o_rows = [padded(n + BLOCK) for n in counts]
        g_rows = padded(pl.cdiv(width, LANES) * tok)
        any_spec = pl.BlockSpec(memory_space=pl.ANY)
        dma = pltpu.SemaphoreType.DMA

        def per_chunk(slots, rows):
            return [pltpu.VMEM((slots, n, LANES), BF16) for n in rows]

        n_chunk = len(chunks)
        return pl.pallas_call(
            functools.partial(kernel, n_head, chunks),
            out_shape=jax.ShapeDtypeStruct((tok, width), BF16),
            in_specs=[any_spec] * 9,
            out_specs=pl.BlockSpec(memory_space=pltpu.VMEM),
            scratch_shapes=[
                pltpu.SMEM(patch_layout.shape, jnp.int32),
                pltpu.SMEM((tok // BLOCK, 2, heads), jnp.int32),
                pltpu.SMEM((1,), jnp.int32),
                pltpu.VMEM((tok, channels), BF16),
                pltpu.VMEM((tok, channels), BF16),
                pltpu.VMEM((tok, channels), BF16),
                pltpu.VMEM(cache_table.shape[1:], BF16),
                pltpu.VMEM((channels, dout // 2), BF16),
                pltpu.VMEM(gate_table.shape, F32),
                per_chunk(ny, q_rows),
                per_chunk(nxz, [2 * n for n in counts]),
                per_chunk(ny, o_rows),
                per_chunk(ny, o_rows),
                per_chunk(2, q_rows),
                pltpu.VMEM((2 * tok, dout // 2), F32),
                pltpu.VMEM((n_head, g_rows, LANES), BF16),
                pltpu.VMEM((n_head, g_rows, LANES), BF16),
                dma((9,)),
                dma((n_chunk, ny)),
                dma((n_chunk, ny)),
                dma((n_chunk, nxz)),
                dma((n_chunk, nxz)),
                dma((n_chunk, ny)),
                dma((n_chunk, ny)),
                dma((n_chunk,)),
                dma((n_chunk,)),
                dma((n_head,)),
                dma((n_head,)),
            ],
            compiler_params=pltpu.CompilerParams(
                collective_id=0, has_side_effects=True, vmem_limit_bytes=60 * 2**20
            ),
        )(
            patch_layout,
            jnp.transpose(exponents[0], (1, 0, 2)),
            timestep,
            queries[0],
            keys_new[0],
            values_new[0],
            cache_table[0],
            out_weight,
            gate_table,
        )

    in_specs = (
        P("cfg", "patch", "head"),
        P("cfg", "patch", "head"),
        P("cfg", "patch", "head"),
        P("cfg", None, None, "head"),
        P("cfg", None, "patch", "head"),
        P(),
        P("head", None),
        P(None, ("cfg", "head")),
        P(),
    )
    out_specs = P("patch", ("cfg", "head"))
    return jax.shard_map(local, mesh=mesh, in_specs=in_specs, out_specs=out_specs, check_vma=False)
```

time: 42.9 us -> 40.1 us (0.935)
  Pallas kernels: 39.3 us -> 37.9 us
  local copies, waits for them, and re-layouts: 2.61 us -> 1.33 us
    pallas_call x1, Pallas kernels: 39.3 us -> 37.9 us  [local(): pl.pallas_call(functools.partial(kernel, n_head, chunks), out_shape=jax.S...]
    unnamed x2 -> x1, local copies, waits for them, and re-layouts: 2.02 us -> 1.33 us
    reshape x1 -> x0, local copies, waits for them, and re-layouts: 0.6 us -> none  [local(): exponents.reshape(-1)]
where the time goes in v2:
time: 40.1 us; the launch traced here: 39.9 us
  Pallas kernels  37.9 us (95%)
  local copies, waits for them, and re-layouts  1.33 us (3%)
  between operations  0.66 us (2%)
    pallas_call x1, Pallas kernels, local(): pl.pallas_call(functools.partial(kernel, n_head, chunks), out_shape=jax.S...  37.9 us
    unnamed x1, local copies, waits for them, and re-layouts  1.33 us

profile of v2, /device:TPU:1, one launch (start us, length us, event | category | flops | bytes accessed | tf_op | source)
XLA Modules:
  0.0 39.9 jit_solution(3453954559202592266)
XLA Ops:
  0.7 37.9 %shard_map.91 = bf16[24,320]{1,0:T(8,128)(2,1)} custom-call(s32[1536]{0:T(1024)} %layout_in.1, s32[3,2,5]{2,1,0:T(2,128)} %bitcast.11, s32[1]{0:T(128)S(6)} %copy.11.timestep_in, bf16[24,640]{1,0:T(8,128)(2,1)} %bitcast.8, bf16[24,640]{1,0:T(8,128)(2,1)} %bitcast.9, bf16[24,640]{1,0:T(8,128)(2,1)} %bitcast.10, bf16[2,256,640]{2,1,0:T(8,128)(2,1)} %bitcast.7, ...), custom_call_target="tpu_custom_call" | custom-call | tf_op jit(solution)/shard_map/pallas_call | solution.py:347
  38.6 1.3 %copy.12 = bf16[24,320]{1,0:T(8,128)(2,1)} copy(bf16[24,320]{1,0:T(8,128)(2,1)} %shard_map.91) | data formatting | bytes 30720

commit v3 on v2

--- a/solution.py
+++ b/solution.py
@@ -243,6 +243,21 @@
 
     for copy in local[6:]:
         copy.wait()
+    def project(c):
+        first, last = chunks[c]
+        a_sends[c].wait_recv()
+        own_a = a_buf[c][0].astype(F32)
+        other_a = a_buf[c][1].astype(F32)
+        stacked = []
+        for h in range(last - first):
+            part = slice(h * tok, (h + 1) * tok)
+            stacked.append(jnp.concatenate([own_a[part], other_a[part]], axis=0))
+        return jnp.dot(
+            jnp.concatenate(stacked, axis=1).astype(BF16),
+            weight[first * LANES : last * LANES, :],
+            preferred_element_type=F32,
+        )
+
     a_sends = []
     for c, (first, last) in enumerate(chunks):
         for copy in o_sends[c]:
@@ -263,23 +278,11 @@
         extra = a_buf[c].shape[1] - rows
         pad = [jnp.zeros((extra, LANES), F32)] if extra else []
         a_buf[c][0] = jnp.concatenate([attended] + pad, axis=0).astype(BF16)
-        swap = send(a_buf[c].at[0], a_buf[c].at[1], a_ssem.at[c], a_rsem.at[c], other_core)
-        a_sends.append(swap)
-        swap.wait_recv()
-        own_a = a_buf[c][0].astype(F32)
-        other_a = a_buf[c][1].astype(F32)
-        stacked = []
-        for h in range(last - first):
-            part = slice(h * tok, (h + 1) * tok)
-            stacked.append(jnp.concatenate([own_a[part], other_a[part]], axis=0))
-        product = jnp.dot(
-            jnp.concatenate(stacked, axis=1).astype(BF16),
-            weight[first * LANES : last * LANES, :],
-            preferred_element_type=F32,
-        )
-        if c < len(chunks) - 1:
-            projected[...] = product if c == 0 else projected[...] + product
-    product = product + projected[...]
+        a_sends.append(send(a_buf[c].at[0], a_buf[c].at[1], a_ssem.at[c], a_rsem.at[c], other_core))
+        if c > 0:
+            product = project(c - 1)
+            projected[...] = product if c == 1 else projected[...] + product
+    product = project(len(chunks) - 1) + projected[...]
     own_p, other_p = product[:tok], product[tok:]
     conditional = jnp.where(cfg == 0, own_p, other_p)
     unconditional = jnp.where(cfg == 0, other_p, own_p)
@@ -332,7 +335,7 @@
         heads = channels // LANES
         dout = out_weight.shape[1]
         width = dout // 2 // n_head
-        chunks = [(0, (heads + 1) // 2), ((heads + 1) // 2, heads)]
+        chunks = [(0, heads // 2), (heads // 2, heads)]
         counts = [(last - first) * tok for first, last in chunks]
         q_rows = [padded(n) for n in counts]
         o_rows = [padded(n + BLOCK) for n in counts]
@@ -346,7 +349,7 @@
         n_chunk = len(chunks)
         return pl.pallas_call(
             functools.partial(kernel, n_head, chunks),
-            out_shape=jax.ShapeDtypeStruct((tok, width), BF16),
+            out_shape=pltpu.VMEM((tok, width), BF16),
             in_specs=[any_spec] * 9,
             out_specs=pl.BlockSpec(memory_space=pltpu.VMEM),
             scratch_shapes=[

time: 40.1 us -> 38.1 us (0.950)
  Pallas kernels: 37.9 us -> 36.7 us
  local copies, waits for them, and re-layouts: 1.33 us -> 0.61 us
    pallas_call x1, Pallas kernels: 37.9 us -> 36.7 us  [local(): pl.pallas_call(functools.partial(kernel, n_head, chunks), out_shape=pltpu...]
    unnamed x1, local copies, waits for them, and re-layouts: 1.33 us -> 0.61 us
where the time goes in v3:
time: 38.1 us; the launch traced here: 38 us
  Pallas kernels  36.7 us (96%)
  between operations  0.66 us (2%)
  local copies, waits for them, and re-layouts  0.61 us (2%)
    pallas_call x1, Pallas kernels, local(): pl.pallas_call(functools.partial(kernel, n_head, chunks), out_shape=pltpu...  36.7 us

profile of v3, /device:TPU:1, one launch (start us, length us, event | category | flops | bytes accessed | tf_op | source)
XLA Modules:
  0.0 38.0 jit_solution(3059583852803551953)
XLA Ops:
  0.7 36.7 %shard_map.91 = bf16[24,320]{1,0:T(8,128)(2,1)S(1)} custom-call(s32[1536]{0:T(1024)} %layout_in.1, s32[3,2,5]{2,1,0:T(2,128)} %bitcast.11, s32[1]{0:T(128)S(6)} %copy.12.timestep_in, bf16[24,640]{1,0:T(8,128)(2,1)} %bitcast.8, bf16[24,640]{1,0:T(8,128)(2,1)} %bitcast.9, bf16[24,640]{1,0:T(8,128)(2,1)} %bitcast.10, bf16[2,256,640]{2,1,0:T(8,128)(2,1)} %bitcast.7, ...), custom_call_target="tpu_custom_call" | custom-call | tf_op jit(solution)/shard_map/pallas_call | solution.py:350
  37.4 0.6 %copy.11 = bf16[24,320]{1,0:T(8,128)(2,1)} copy(bf16[24,320]{1,0:T(8,128)(2,1)S(1)} %shard_map.91) | data formatting | bytes 30720

commit v4 on v2

--- a/solution.py
+++ b/solution.py
@@ -55,7 +55,6 @@
     kv_all,
     o_send,
     o_recv,
-    a_buf,
     projected,
     g_send,
     g_recv,
@@ -66,8 +65,6 @@
     kv_rsem,
     o_ssem,
     o_rsem,
-    a_ssem,
-    a_rsem,
     g_ssem,
     g_rsem,
 ):
@@ -76,7 +73,6 @@
     tok = q_in.shape[0]
     heads = q_in.shape[1] // LANES
     blocks = tok // BLOCK
-    half = weight.shape[1]
     width = out.shape[1]
 
     cfg = lax.axis_index("cfg")
@@ -95,8 +91,8 @@
         other_x = lax.rem(x + dx, nx)
         return (cfg, (other_z * nx + other_x) * ny + y, head)
 
-    def head_partner(step):
-        return (cfg, patch, lax.rem(head + step, n_head))
+    def feature_partner(swap, step):
+        return (1 - cfg if swap else cfg, patch, lax.rem(head + step, n_head))
 
     def send(src, dst, ssem, rsem, device):
         copy = pltpu.make_async_remote_copy(
@@ -110,18 +106,14 @@
         copy.start()
         return copy
 
-    other_core = (1 - cfg, patch, head)
     y_steps = far_first(ny)
     xz_steps = [(1, dx) for dx in far_first(nx)] if nz > 1 else []
     xz_steps += [(0, dx) for dx in far_first(nx)]
     xz_steps += [(1, 0)] if nz > 1 else []
-    head_steps = far_first(n_head)
+    feature_steps = [(swap, s) for s in far_first(n_head) for swap in (0, 1)] + [(1, 0)]
 
     partners = [y_partner(s) for s in y_steps] + [xz_partner(*s) for s in xz_steps]
-    partners += [head_partner(s) for s in head_steps] + [other_core]
-    barrier = pltpu.get_barrier_semaphore()
-    for partner in partners:
-        pl.semaphore_signal(barrier, inc=1, device_id=partner, device_id_type=MESH)
+    partners += [feature_partner(*s) for s in feature_steps]
     pairs = [
         (queries, q_in),
         (layout_in, layout),
@@ -131,11 +123,14 @@
         (values_new, v_in),
         (timestep_in, timestep),
         (gate_table, gate),
-        (out_weight.at[:, pl.ds(pl.multiple_of(cfg * half, LANES), half)], weight),
+        (out_weight, weight),
     ]
     local = [pltpu.make_async_copy(a, b, local_sem.at[i]) for i, (a, b) in enumerate(pairs)]
     for copy in local[:6]:
         copy.start()
+    barrier = pltpu.get_barrier_semaphore()
+    for partner in partners:
+        pl.semaphore_signal(barrier, inc=1, device_id=partner, device_id_type=MESH)
 
     local[0].wait()
     own_q = q_in[...].astype(F32)
@@ -178,17 +173,16 @@
 
     pl.semaphore_wait(barrier, len(partners))
 
-    gathers = []
-    for c in range(len(chunks)):
-        copies = []
-        for y_step, xz_step in zip(y_steps, xz_steps):
-            q, kv = q_all[c], kv_all[c]
-            slot = xz_step[0] * nx + xz_step[1]
-            copies += [
-                send(q.at[0], q.at[y_step], q_ssem.at[c, y_step], q_rsem.at[c, y_step], y_partner(y_step)),
-                send(kv.at[0], kv.at[slot], kv_ssem.at[c, slot], kv_rsem.at[c, slot], xz_partner(*xz_step)),
-            ]
-        gathers.append(copies)
+    gathers = [[] for _ in chunks]
+    for c, q in enumerate(q_all):
+        for s in y_steps:
+            copy = send(q.at[0], q.at[s], q_ssem.at[c, s], q_rsem.at[c, s], y_partner(s))
+            gathers[c].append(copy)
+    for c, kv in enumerate(kv_all):
+        for dz, dx in xz_steps:
+            e = dz * nx + dx
+            copy = send(kv.at[0], kv.at[e], kv_ssem.at[c, e], kv_rsem.at[c, e], xz_partner(dz, dx))
+            gathers[c].append(copy)
     for copy in local[6:]:
         copy.start()
 
@@ -243,7 +237,6 @@
 
     for copy in local[6:]:
         copy.wait()
-    a_sends = []
     for c, (first, last) in enumerate(chunks):
         for copy in o_sends[c]:
             copy.wait_recv()
@@ -260,55 +253,59 @@
         for o, share in zip(o_f, shares):
             column = jnp.sum(jnp.where(eye, share / total, 0.0), axis=1, keepdims=True)
             attended = attended + o[:rows] * column
-        extra = a_buf[c].shape[1] - rows
-        pad = [jnp.zeros((extra, LANES), F32)] if extra else []
-        a_buf[c][0] = jnp.concatenate([attended] + pad, axis=0).astype(BF16)
-        swap = send(a_buf[c].at[0], a_buf[c].at[1], a_ssem.at[c], a_rsem.at[c], other_core)
-        a_sends.append(swap)
-        swap.wait_recv()
-        own_a = a_buf[c][0].astype(F32)
-        other_a = a_buf[c][1].astype(F32)
-        stacked = []
-        for h in range(last - first):
-            part = slice(h * tok, (h + 1) * tok)
-            stacked.append(jnp.concatenate([own_a[part], other_a[part]], axis=0))
+        by_head = [attended[h * tok : (h + 1) * tok] for h in range(last - first)]
         product = jnp.dot(
-            jnp.concatenate(stacked, axis=1).astype(BF16),
+            jnp.concatenate(by_head, axis=1).astype(BF16),
             weight[first * LANES : last * LANES, :],
             preferred_element_type=F32,
         )
+        if c > 0:
+            product = product + projected[...]
         if c < len(chunks) - 1:
-            projected[...] = product if c == 0 else projected[...] + product
-    product = product + projected[...]
-    own_p, other_p = product[:tok], product[tok:]
-    conditional = jnp.where(cfg == 0, own_p, other_p)
-    unconditional = jnp.where(cfg == 0, other_p, own_p)
-    mixed = unconditional + 5.0 * (conditional - unconditional)
-
-    n_cols = pl.cdiv(width, LANES)
-    mixed = jnp.concatenate([mixed, jnp.zeros((tok, LANES), F32)], axis=1)
-    extra = g_send.shape[1] - n_cols * tok
-    pad = [jnp.zeros((extra, LANES), F32)] if extra else []
-    for k in range(n_head):
-        starts = [k * width + i * LANES for i in range(n_cols)]
-        g_send[k] = jnp.concatenate([mixed[:, i : i + LANES] for i in starts] + pad, axis=0).astype(BF16)
-    g_sends = [
-        send(g_send.at[lax.rem(head + s, n_head)], g_recv.at[s], g_ssem.at[s], g_rsem.at[s], head_partner(s))
-        for s in head_steps
-    ]
+            projected[...] = product
+
+    product = product * jnp.where(cfg == 0, 5.0, -4.0)
+    n_full, rest = width // LANES, width % LANES
+    lane16 = lax.broadcasted_iota(jnp.int32, (2 * BLOCK, LANES), 1)
+    for k in range(2 * n_head):
+        first = k * width // LANES
+        odd = k % 2
+        tile = first if odd else first + n_full
+        half = product[:, tile * LANES : (tile + 1) * LANES]
+        beside = jnp.concatenate([half[2 * BLOCK :], jnp.zeros((BLOCK, LANES), F32)], axis=0)
+        own_lanes = lane16 >= rest if odd else lane16 < rest
+        packed = jnp.where(own_lanes, half[: 2 * BLOCK], pltpu.roll(beside, rest, 1))
+        pieces = [
+            product[:, (first + odd + i) * LANES : (first + odd + i + 1) * LANES] for i in range(n_full)
+        ]
+        g_send[k] = jnp.concatenate(pieces + [packed], axis=0).astype(BF16)
+    own_block = cfg * n_head + head
+    g_sends = []
+    for swap, s in feature_steps:
+        slot = swap * n_head + s
+        block = (1 - cfg if swap else cfg) * n_head + lax.rem(head + s, n_head)
+        g_sends.append(
+            send(g_send.at[block], g_recv.at[slot], g_ssem.at[slot], g_rsem.at[slot], feature_partner(swap, s))
+        )
     here = lax.broadcasted_iota(jnp.int32, gate.shape, 0) == timestep[0]
     gate_row = jnp.sum(jnp.where(here, gate[...], 0.0), axis=0, keepdims=True)
-    summed = g_send[head].astype(F32)
-    for s, copy in zip(head_steps, g_sends):
+    summed = g_send[own_block].astype(F32)
+    for (swap, s), copy in zip(feature_steps, g_sends):
         copy.wait_recv()
-        summed = summed + g_recv[s].astype(F32)
-    for i in range(n_cols):
-        lanes = min(LANES, width - i * LANES)
-        cols = slice(i * LANES, i * LANES + lanes)
-        part = summed[i * tok : (i + 1) * tok, :lanes] * gate_row[:, cols]
-        out[:, cols] = part.astype(out.dtype)
-
-    for copy in sum(gathers + o_sends, []) + a_sends + g_sends:
+        summed = summed + g_recv[swap * n_head + s].astype(F32)
+    whole = [summed[i * tok : (i + 1) * tok] for i in range(n_full)]
+    packed = summed[n_full * tok :]
+    turned = pltpu.roll(packed, rest, 1)
+    low = jnp.concatenate([packed, turned[:BLOCK]], axis=0)[:, :rest]
+    high = jnp.concatenate([turned, packed[:BLOCK]], axis=0)[:, :rest]
+    total = jnp.where(
+        lax.rem(head, 2) == 0,
+        jnp.concatenate(whole + [low], axis=1),
+        jnp.concatenate([high] + whole, axis=1),
+    )
+    out[...] = (total * gate_row).astype(out.dtype)
+
+    for copy in sum(gathers + o_sends, []) + g_sends:
         copy.wait_send()
 
 
@@ -332,11 +329,11 @@
         heads = channels // LANES
         dout = out_weight.shape[1]
         width = dout // 2 // n_head
-        chunks = [(0, (heads + 1) // 2), ((heads + 1) // 2, heads)]
+        chunks = [(0, heads // 2), (heads // 2, heads)]
         counts = [(last - first) * tok for first, last in chunks]
         q_rows = [padded(n) for n in counts]
         o_rows = [padded(n + BLOCK) for n in counts]
-        g_rows = padded(pl.cdiv(width, LANES) * tok)
+        g_rows = width // LANES * tok + 2 * BLOCK
         any_spec = pl.BlockSpec(memory_space=pl.ANY)
         dma = pltpu.SemaphoreType.DMA
 
@@ -346,7 +343,7 @@
         n_chunk = len(chunks)
         return pl.pallas_call(
             functools.partial(kernel, n_head, chunks),
-            out_shape=jax.ShapeDtypeStruct((tok, width), BF16),
+            out_shape=pltpu.VMEM((tok, width), BF16),
             in_specs=[any_spec] * 9,
             out_specs=pl.BlockSpec(memory_space=pltpu.VMEM),
             scratch_shapes=[
@@ -357,16 +354,15 @@
                 pltpu.VMEM((tok, channels), BF16),
                 pltpu.VMEM((tok, channels), BF16),
                 pltpu.VMEM(cache_table.shape[1:], BF16),
-                pltpu.VMEM((channels, dout // 2), BF16),
+                pltpu.VMEM((channels, dout), BF16),
                 pltpu.VMEM(gate_table.shape, F32),
                 per_chunk(ny, q_rows),
                 per_chunk(nxz, [2 * n for n in counts]),
                 per_chunk(ny, o_rows),
                 per_chunk(ny, o_rows),
-                per_chunk(2, q_rows),
-                pltpu.VMEM((2 * tok, dout // 2), F32),
-                pltpu.VMEM((n_head, g_rows, LANES), BF16),
-                pltpu.VMEM((n_head, g_rows, LANES), BF16),
+                pltpu.VMEM((tok, dout), F32),
+                pltpu.VMEM((2 * n_head, g_rows, LANES), BF16),
+                pltpu.VMEM((2 * n_head, g_rows, LANES), BF16),
                 dma((9,)),
                 dma((n_chunk, ny)),
                 dma((n_chunk, ny)),
@@ -374,10 +370,8 @@
                 dma((n_chunk, nxz)),
                 dma((n_chunk, ny)),
                 dma((n_chunk, ny)),
-                dma((n_chunk,)),
-                dma((n_chunk,)),
-                dma((n_head,)),
-                dma((n_head,)),
+                dma((2 * n_head,)),
+                dma((2 * n_head,)),
             ],
             compiler_params=pltpu.CompilerParams(
                 collective_id=0, has_side_effects=True, vmem_limit_bytes=60 * 2**20

time: 40.1 us -> 37.5 us (0.935)
  Pallas kernels: 37.9 us -> 35.9 us
  local copies, waits for them, and re-layouts: 1.33 us -> 0.61 us
    pallas_call x1, Pallas kernels: 37.9 us -> 35.9 us  [local(): pl.pallas_call(functools.partial(kernel, n_head, chunks), out_shape=pltpu...]
    unnamed x1, local copies, waits for them, and re-layouts: 1.33 us -> 0.61 us
where the time goes in v4:
time: 37.5 us; the launch traced here: 37.2 us
  Pallas kernels  35.9 us (96%)
  between operations  0.66 us (2%)
  local copies, waits for them, and re-layouts  0.61 us (2%)
    pallas_call x1, Pallas kernels, local(): pl.pallas_call(functools.partial(kernel, n_head, chunks), out_shape=pltpu...  35.9 us

profile of v4, /device:TPU:1, one launch (start us, length us, event | category | flops | bytes accessed | tf_op | source)
XLA Modules:
  0.0 37.2 jit_solution(223777530806385587)
XLA Ops:
  0.7 35.9 %shard_map.91 = bf16[24,320]{1,0:T(8,128)(2,1)S(1)} custom-call(s32[1536]{0:T(1024)} %layout_in.1, s32[3,2,5]{2,1,0:T(2,128)} %bitcast.11, s32[1]{0:T(128)S(6)} %copy.12.timestep_in, bf16[24,640]{1,0:T(8,128)(2,1)} %bitcast.8, bf16[24,640]{1,0:T(8,128)(2,1)} %bitcast.9, bf16[24,640]{1,0:T(8,128)(2,1)} %bitcast.10, bf16[2,256,640]{2,1,0:T(8,128)(2,1)} %bitcast.7, ...), custom_call_target="tpu_custom_call" | custom-call | tf_op jit(solution)/shard_map/pallas_call | solution.py:344
  36.6 0.6 %copy.11 = bf16[24,320]{1,0:T(8,128)(2,1)} copy(bf16[24,320]{1,0:T(8,128)(2,1)S(1)} %shard_map.91) | data formatting | bytes 30720

commit v5 on v4

--- a/solution.py
+++ b/solution.py
@@ -110,7 +110,7 @@
     xz_steps = [(1, dx) for dx in far_first(nx)] if nz > 1 else []
     xz_steps += [(0, dx) for dx in far_first(nx)]
     xz_steps += [(1, 0)] if nz > 1 else []
-    feature_steps = [(swap, s) for s in far_first(n_head) for swap in (0, 1)] + [(1, 0)]
+    feature_steps = [(swap, s) for s in far_first(n_head) for swap in (1, 0)] + [(1, 0)]
 
     partners = [y_partner(s) for s in y_steps] + [xz_partner(*s) for s in xz_steps]
     partners += [feature_partner(*s) for s in feature_steps]
@@ -259,37 +259,35 @@
             weight[first * LANES : last * LANES, :],
             preferred_element_type=F32,
         )
-        if c > 0:
-            product = product + projected[...]
-        if c < len(chunks) - 1:
-            projected[...] = product
-
-    product = product * jnp.where(cfg == 0, 5.0, -4.0)
+        projected[...] = product if c == 0 else projected[...] + product
+
+    coefficient = jnp.where(cfg == 0, 5.0, -4.0)
     n_full, rest = width // LANES, width % LANES
     lane16 = lax.broadcasted_iota(jnp.int32, (2 * BLOCK, LANES), 1)
-    for k in range(2 * n_head):
-        first = k * width // LANES
-        odd = k % 2
-        tile = first if odd else first + n_full
-        half = product[:, tile * LANES : (tile + 1) * LANES]
+
+    def features(swap, step):
+        block = (1 - cfg if swap else cfg) * n_head + lax.rem(head + step, n_head)
+        odd = lax.rem(block, 2) == 1
+        start = pl.multiple_of(block * width // LANES * LANES, LANES)
+        term = projected[:, pl.ds(start, (n_full + 1) * LANES)] * coefficient
+        tiles = [term[:, i * LANES : (i + 1) * LANES] for i in range(n_full + 1)]
+        half = jnp.where(odd, tiles[0], tiles[-1])
         beside = jnp.concatenate([half[2 * BLOCK :], jnp.zeros((BLOCK, LANES), F32)], axis=0)
-        own_lanes = lane16 >= rest if odd else lane16 < rest
+        own_lanes = (lane16 >= rest) == odd
         packed = jnp.where(own_lanes, half[: 2 * BLOCK], pltpu.roll(beside, rest, 1))
-        pieces = [
-            product[:, (first + odd + i) * LANES : (first + odd + i + 1) * LANES] for i in range(n_full)
-        ]
-        g_send[k] = jnp.concatenate(pieces + [packed], axis=0).astype(BF16)
-    own_block = cfg * n_head + head
+        pieces = [jnp.where(odd, tiles[i + 1], tiles[i]) for i in range(n_full)]
+        return jnp.concatenate(pieces + [packed], axis=0)
+
     g_sends = []
     for swap, s in feature_steps:
         slot = swap * n_head + s
-        block = (1 - cfg if swap else cfg) * n_head + lax.rem(head + s, n_head)
+        g_send[slot] = features(swap, s).astype(BF16)
         g_sends.append(
-            send(g_send.at[block], g_recv.at[slot], g_ssem.at[slot], g_rsem.at[slot], feature_partner(swap, s))
+            send(g_send.at[slot], g_recv.at[slot], g_ssem.at[slot], g_rsem.at[slot], feature_partner(swap, s))
         )
     here = lax.broadcasted_iota(jnp.int32, gate.shape, 0) == timestep[0]
     gate_row = jnp.sum(jnp.where(here, gate[...], 0.0), axis=0, keepdims=True)
-    summed = g_send[own_block].astype(F32)
+    summed = features(0, 0)
     for (swap, s), copy in zip(feature_steps, g_sends):
         copy.wait_recv()
         summed = summed + g_recv[swap * n_head + s].astype(F32)

time: 37.5 us -> 37.2 us (level)
  no operation moved by 1% of the time
where the time goes in v5:
time: 37.2 us; the launch traced here: 37 us
  Pallas kernels  35.7 us (96%)
  between operations  0.66 us (2%)
  local copies, waits for them, and re-layouts  0.61 us (2%)
    pallas_call x1, Pallas kernels, local(): pl.pallas_call(functools.partial(kernel, n_head, chunks), out_shape=pltpu...  35.7 us

profile of v5, /device:TPU:1, one launch (start us, length us, event | category | flops | bytes accessed | tf_op | source)
XLA Modules:
  0.0 37.0 jit_solution(6539800931054615437)
XLA Ops:
  0.7 35.7 %shard_map.91 = bf16[24,320]{1,0:T(8,128)(2,1)S(1)} custom-call(s32[1536]{0:T(1024)} %layout_in.1, s32[3,2,5]{2,1,0:T(2,128)} %bitcast.11, s32[1]{0:T(128)S(6)} %copy.12.timestep_in, bf16[24,640]{1,0:T(8,128)(2,1)} %bitcast.8, bf16[24,640]{1,0:T(8,128)(2,1)} %bitcast.9, bf16[24,640]{1,0:T(8,128)(2,1)} %bitcast.10, bf16[2,256,640]{2,1,0:T(8,128)(2,1)} %bitcast.7, ...), custom_call_target="tpu_custom_call" | custom-call | tf_op jit(solution)/shard_map/pallas_call | solution.py:342
  36.4 0.6 %copy.11 = bf16[24,320]{1,0:T(8,128)(2,1)} copy(bf16[24,320]{1,0:T(8,128)(2,1)S(1)} %shard_map.91) | data formatting | bytes 30720

commit v6 on v5

--- a/solution.py
+++ b/solution.py
@@ -118,15 +118,16 @@
         (queries, q_in),
         (layout_in, layout),
         (exponents_in, exponents),
-        (cache_table, table),
         (keys_new, k_in),
+        (cache_table.at[0], table.at[0]),
         (values_new, v_in),
+        (cache_table.at[1], table.at[1]),
         (timestep_in, timestep),
         (gate_table, gate),
         (out_weight, weight),
     ]
     local = [pltpu.make_async_copy(a, b, local_sem.at[i]) for i, (a, b) in enumerate(pairs)]
-    for copy in local[:6]:
+    for copy in local[:7]:
         copy.start()
     barrier = pltpu.get_barrier_semaphore()
     for partner in partners:
@@ -151,10 +152,11 @@
         picks.append(jnp.where(lane == wanted, 1.0, 0.0).astype(F32))
     onehot = jnp.concatenate(picks, axis=0).astype(BF16)
 
-    for copy in local[2:6]:
-        copy.wait()
+    local[2].wait()
     full = [[], []]
     for kind, fresh_ref in enumerate((k_in, v_in)):
+        local[3 + 2 * kind].wait()
+        local[4 + 2 * kind].wait()
         cached = jnp.dot(onehot, table[kind], preferred_element_type=F32)
         fresh = fresh_ref[...].astype(F32)
         for h in range(heads):
@@ -183,7 +185,7 @@
             e = dz * nx + dx
             copy = send(kv.at[0], kv.at[e], kv_ssem.at[c, e], kv_rsem.at[c, e], xz_partner(dz, dx))
             gathers[c].append(copy)
-    for copy in local[6:]:
+    for copy in local[7:]:
         copy.start()
 
     inverse_root = 1.0 / math.sqrt(LANES)
@@ -235,7 +237,7 @@
                 )
         o_sends.append(copies)
 
-    for copy in local[6:]:
+    for copy in local[7:]:
         copy.wait()
     for c, (first, last) in enumerate(chunks):
         for copy in o_sends[c]:
@@ -361,7 +363,7 @@
                 pltpu.VMEM((tok, dout), F32),
                 pltpu.VMEM((2 * n_head, g_rows, LANES), BF16),
                 pltpu.VMEM((2 * n_head, g_rows, LANES), BF16),
-                dma((9,)),
+                dma((10,)),
                 dma((n_chunk, ny)),
                 dma((n_chunk, ny)),
                 dma((n_chunk, nxz)),

time: 37.2 us -> 37.4 us (level)
  no operation moved by 1% of the time
where the time goes in v6:
time: 37.4 us; the launch traced here: 37.3 us
  Pallas kernels  36 us (96%)
  between operations  0.66 us (2%)
  local copies, waits for them, and re-layouts  0.61 us (2%)
    pallas_call x1, Pallas kernels, local(): pl.pallas_call(functools.partial(kernel, n_head, chunks), out_shape=pltpu...  36 us

profile of v6, /device:TPU:1, one launch (start us, length us, event | category | flops | bytes accessed | tf_op | source)
XLA Modules:
  0.0 37.3 jit_solution(3860949115065122245)
XLA Ops:
  0.7 36.0 %shard_map.91 = bf16[24,320]{1,0:T(8,128)(2,1)S(1)} custom-call(s32[1536]{0:T(1024)} %layout_in.1, s32[3,2,5]{2,1,0:T(2,128)} %bitcast.11, s32[1]{0:T(128)S(6)} %copy.12.timestep_in, bf16[24,640]{1,0:T(8,128)(2,1)} %bitcast.8, bf16[24,640]{1,0:T(8,128)(2,1)} %bitcast.9, bf16[24,640]{1,0:T(8,128)(2,1)} %bitcast.10, bf16[2,256,640]{2,1,0:T(8,128)(2,1)} %bitcast.7, ...), custom_call_target="tpu_custom_call" | custom-call | tf_op jit(solution)/shard_map/pallas_call | solution.py:344
  36.7 0.6 %copy.11 = bf16[24,320]{1,0:T(8,128)(2,1)} copy(bf16[24,320]{1,0:T(8,128)(2,1)S(1)} %shard_map.91) | data formatting | bytes 30720

commit v7 on v5

--- a/solution.py
+++ b/solution.py
@@ -107,9 +107,7 @@
         return copy
 
     y_steps = far_first(ny)
-    xz_steps = [(1, dx) for dx in far_first(nx)] if nz > 1 else []
-    xz_steps += [(0, dx) for dx in far_first(nx)]
-    xz_steps += [(1, 0)] if nz > 1 else []
+    xz_steps = [(1, 2), (0, 2), (1, 1), (1, 3), (0, 1), (0, 3), (1, 0)]
     feature_steps = [(swap, s) for s in far_first(n_head) for swap in (1, 0)] + [(1, 0)]
 
     partners = [y_partner(s) for s in y_steps] + [xz_partner(*s) for s in xz_steps]

time: 37.2 us -> 37.4 us (level)
  no operation moved by 1% of the time
where the time goes in v7:
time: 37.4 us; the launch traced here: 37.3 us
  Pallas kernels  36 us (96%)
  between operations  0.66 us (2%)
  local copies, waits for them, and re-layouts  0.61 us (2%)
    pallas_call x1, Pallas kernels, local(): pl.pallas_call(functools.partial(kernel, n_head, chunks), out_shape=pltpu...  36 us

profile of v7, /device:TPU:1, one launch (start us, length us, event | category | flops | bytes accessed | tf_op | source)
XLA Modules:
  0.0 37.3 jit_solution(9284320418809180243)
XLA Ops:
  0.7 36.0 %shard_map.91 = bf16[24,320]{1,0:T(8,128)(2,1)S(1)} custom-call(s32[1536]{0:T(1024)} %layout_in.1, s32[3,2,5]{2,1,0:T(2,128)} %bitcast.11, s32[1]{0:T(128)S(6)} %copy.12.timestep_in, bf16[24,640]{1,0:T(8,128)(2,1)} %bitcast.8, bf16[24,640]{1,0:T(8,128)(2,1)} %bitcast.9, bf16[24,640]{1,0:T(8,128)(2,1)} %bitcast.10, bf16[2,256,640]{2,1,0:T(8,128)(2,1)} %bitcast.7, ...), custom_call_target="tpu_custom_call" | custom-call | tf_op jit(solution)/shard_map/pallas_call | solution.py:340
  36.7 0.6 %copy.11 = bf16[24,320]{1,0:T(8,128)(2,1)} copy(bf16[24,320]{1,0:T(8,128)(2,1)S(1)} %shard_map.91) | data formatting | bytes 30720
